TPU v7x, 256 devices: a whole 4x4x8 slice. The times are simulated.
256 devices in a mesh: dom: 32 (over y, x, core), blk: 8 (over z).
Axes of the slice: x: 4, y: 4, z: 8, core: 2. Of those that a mesh axis runs over, the one named last changes fastest.
Arguments:
- source: bfloat16 [4096, 192], P(('dom', 'blk')), may hold values from -6 to 6
- lam_init: bfloat16 [4096, 192], P(('dom', 'blk')), may hold values from -6 to 6
- offd: bfloat16 [4096, 192, 1152], P(('dom', 'blk')), may hold values from -0.1875 to 0.1875
- dinv: bfloat16 [192, 786432], P(None, ('dom', 'blk')), may hold values from -0.4375 to 0.4375
- colidx: int32 [4096, 6], P(('dom', 'blk')), may hold values from 0 to 191
- face_list: int32 [32, 64], P('dom'), may hold values from 0 to 127
- partner: int32 [32], P('dom'), may hold values from 0 to 31, as said below
- perf_block: int32 [32768], P(('dom', 'blk')), may hold values from 0 to 15
- perf_well: int32 [32768], P(('dom', 'blk')), may hold values from 0 to 63
- perf_sens: bfloat16 [32768, 192], P(('dom', 'blk')), may hold values from -0.21875 to 0.21875
- obj_weight: float32 [1024], replicated, may hold values from 0.5 to 2
- step_index: int32 [1], replicated, may hold values from 0 to 1023
Outputs:
- adjoint: float32 [4096, 192], P(('dom', 'blk'))
- control_grad: float32 [2048], P(('dom', 'blk'))
Inputs may be any that keep to these rules, and one draw needn't show every extreme that they name: Below 128 an own block of the partition, from 128 on halo block colidx - 128. `face_list`: blocks of the partition's own 128, repeats possible. A pairing: partner[p] != p and partner[partner[p]] == p.
All inputs are finite; a program needn't handle non-finite values.
Results may differ from a plain program's by a relative error of at most 0.0054.
Values may be sent and summed in bfloat16 or wider, within the bound.
No kernel may reach another device: no remote copies, remote signals or barrier semaphores. Data moves between devices by JAX's collectives and lax.ppermute only.
A program may use at most 64 MiB of HBM per device.

v0:
```python
import jax
import jax.numpy as jnp
from jax import lax
from jax.sharding import PartitionSpec as P

WP = 64


def cross_partition(face_rows, partner_id):
    slot_count = lax.axis_size("dom")
    onehot = (jnp.arange(slot_count, dtype=jnp.int32) == partner_id).astype(jnp.bfloat16)
    outgoing = onehot[:, None, None] * face_rows[None, :, :]
    incoming = lax.all_to_all(outgoing, "dom", split_axis=0, concat_axis=0, tiled=True)
    halo_blocks = lax.dynamic_index_in_dim(incoming, partner_id, 0, keepdims=False)
    return halo_blocks


def extended_state(state, face_index, partner_id):
    partition = lax.all_gather(state, "blk", axis=0, tiled=True)
    halo_blocks = cross_partition(partition[face_index], partner_id)
    return jnp.concatenate([partition, halo_blocks], axis=0)


def sweep_once(state, forcing, offd, inverses, colidx, face_index, partner_id):
    extended = extended_state(state, face_index, partner_id)
    picked = extended[colidx].reshape(colidx.shape[0], -1)
    coupled = jnp.einsum("bim,bm->bi", offd, picked, preferred_element_type=jnp.float32)
    residual_rhs = (forcing - coupled).astype(jnp.bfloat16)
    return jnp.einsum("ibj,bj->bi", inverses, residual_rhs, preferred_element_type=jnp.float32)


def body(
    source,
    lam_init,
    offd,
    dinv,
    colidx,
    face_list,
    partner,
    perf_block,
    perf_well,
    perf_sens,
    obj_weight,
    step_index,
):
    weight = lax.dynamic_index_in_dim(obj_weight, step_index[0], 0, keepdims=False)
    forcing = weight * source.astype(jnp.float32)
    width = source.shape[1]
    inverses = dinv.reshape(width, source.shape[0], width)
    face_index = face_list[0]
    partner_id = partner[0]
    first_pass = sweep_once(
        lam_init, forcing, offd, inverses, colidx, face_index, partner_id
    ).astype(jnp.bfloat16)
    adjoint = sweep_once(first_pass, forcing, offd, inverses, colidx, face_index, partner_id)
    contrib = jnp.sum(perf_sens.astype(jnp.float32) * adjoint[perf_block], axis=1)
    onehot = (perf_well[:, None] == jnp.arange(WP, dtype=jnp.int32)[None, :]).astype(jnp.float32)
    well_terms = -jnp.dot(contrib, onehot, precision=lax.Precision.HIGHEST)
    control_grad = lax.psum_scatter(well_terms, "blk", scatter_dimension=0, tiled=True)
    return (adjoint, control_grad)


def solution(mesh):
    placed = (
        P(("dom", "blk"), None),
        P(("dom", "blk"), None),
        P(("dom", "blk"), None, None),
        P(None, ("dom", "blk")),
        P(("dom", "blk"), None),
        P("dom", None),
        P("dom"),
        P(("dom", "blk")),
        P(("dom", "blk")),
        P(("dom", "blk"), None),
        P(),
        P(),
    )
    return jax.shard_map(
        body,
        mesh=mesh,
        in_specs=placed,
        out_specs=(P(("dom", "blk"), None), P(("dom", "blk"))),
        check_vma=False,
    )
```

profile of v0, /device:TPU:2, one launch (start us, length us, event | category | flops | bytes accessed | tf_op | source)
XLA Modules:
  0.0 136.8 jit_solution(17076358415785166185)
XLA Ops:
  1.3 28.4 %all_gather.6 = bf16[128,192]{1,0:T(8,128)(2,1)S(1)} all-gather(bf16[16,192]{1,0:T(8,128)(2,1)} %param.13), channel_id=1, replica_groups=mesh['dom'=32,'blk'=8] {'blk'}, dimensions={0}, use_global_device_ids=true | all-gather | bytes 55296 | tf_op jit(solution)/shard_map/all_gather | solution.py:19
  29.7 0.7 fusion.10
  30.3 0.7 gather_fusion
  31.0 0.0 copy-start.4
  31.1 0.0 copy-start.1
  31.1 1.2 broadcast_multiply_fusion.1
  32.2 7.7 %all-to-all-start = ((bf16[32,64,192]{2,1,0:T(8,128)(2,1)}), bf16[32,64,192]{2,1,0:T(8,128)(2,1)}, u32[]{:S(2)}, u32[]{:S(2)}) async-start(bf16[32,64,192]{2,1,0:T(8,128)(2,1)} %broadcast_multiply_fusion.1), calls=%async_computation | async-start | bytes 2097152 | tf_op jit(solution)/shard_map/all_to_all | solution.py:13
  39.9 0.0 copy-done.4
  40.0 0.1 copy.18
  40.0 0.1 reshape.62
  40.8 0.0 copy-done.1
  40.8 0.7 copy.29
  41.5 1.3 dynamic_slice.11
  42.8 13.3 %all-to-all-done = bf16[32,64,192]{2,1,0:T(8,128)(2,1)} async-done(((bf16[32,64,192]{2,1,0:T(8,128)(2,1)}), bf16[32,64,192]{2,1,0:T(8,128)(2,1)}, u32[]{:S(2)}, u32[]{:S(2)}) %all-to-all-start) | async-done | bytes 786464 | tf_op jit(solution)/shard_map/all_to_all | solution.py:13
  56.1 0.8 dynamic-slice_bitcast_fusion.1
  56.9 0.8 gather_fusion.1
  57.7 0.1 reshape.110
  57.8 0.0 copy-start.3
  57.8 5.2 %fusion.12 = f32[16,1,192]{2,1,0:T(1,128)S(1)} fusion(bf16[16,1152,1]{1,2,0:T(2,128)(2,1)S(1)} %reshape.110, bf16[16,192,1152]{2,1,0:T(8,128)(2,1)} %param.14), kind=kOutput, calls=%fused_computation.38 | convolution fusion | flops 7077888 | bytes 7127040 | tf_op jit(solution)/shard_map/bim,bm->bi/dot_general | solution.py:27
  62.9 0.0 copy-done.3
  62.9 0.7 fusion.8
  63.6 0.3 fusion.6
  63.9 24.6 %all_gather.7 = bf16[128,192]{1,0:T(8,128)(2,1)S(1)} all-gather(bf16[16,192]{1,0:T(8,128)(2,1)S(1)} %bitcast.59), channel_id=1, replica_groups=mesh['dom'=32,'blk'=8] {'blk'}, dimensions={0}, use_global_device_ids=true | all-gather | bytes 55296 | tf_op jit(solution)/shard_map/all_gather | solution.py:19
  88.5 0.7 gather_fusion.2
  89.2 0.0 copy-start.2
  89.2 0.0 copy-start.7
  89.2 0.0 copy-start.5
  89.2 1.1 broadcast_multiply_fusion
  90.3 5.0 %all-to-all-start.1 = ((bf16[32,64,192]{2,1,0:T(8,128)(2,1)}), bf16[32,64,192]{2,1,0:T(8,128)(2,1)S(1)}, u32[]{:S(2)}, u32[]{:S(2)}) async-start(bf16[32,64,192]{2,1,0:T(8,128)(2,1)} %broadcast_multiply_fusion), calls=%async_computation.1 | async-start | bytes 2097152 | tf_op jit(solution)/shard_map/all_to_all | solution.py:13
  95.4 0.0 copy-done.2
  95.4 0.1 copy.19
  95.5 0.0 copy-done.7
  95.5 0.6 dynamic-slice
  96.8 0.0 copy-done.5
  96.8 14.8 %all-to-all-done.1 = bf16[32,64,192]{2,1,0:T(8,128)(2,1)S(1)} async-done(((bf16[32,64,192]{2,1,0:T(8,128)(2,1)}), bf16[32,64,192]{2,1,0:T(8,128)(2,1)S(1)}, u32[]{:S(2)}, u32[]{:S(2)}) %all-to-all-start.1) | async-done | bytes 786464 | tf_op jit(solution)/shard_map/all_to_all | solution.py:13
  111.6 0.8 gather_fusion.3
  112.4 0.1 reshape.112
  112.5 5.2 %fusion.13 = f32[16,1,192]{2,1,0:T(1,128)S(1)} fusion(bf16[16,1152,1]{1,2,0:T(2,128)(2,1)S(1)} %reshape.112, bf16[16,192,1152]{2,1,0:T(8,128)(2,1)} %param.14), kind=kOutput, calls=%fused_computation.39 | convolution fusion | flops 7077888 | bytes 7127040 | tf_op jit(solution)/shard_map/bim,bm->bi/dot_general | solution.py:27
  117.7 0.0 copy-start.6
  117.7 0.7 fusion.9
  118.4 0.3 fusion.4
  118.7 0.0 copy-start
  118.7 0.8 gather_fusion.4
  119.5 0.1 multiply_reduce_fusion
  119.6 0.0 copy-done.6
  119.6 0.2 fusion
  119.8 16.4 %all-reduce = f32[64]{0:T(128)S(1)} all-reduce(f32[64]{0:T(128)S(1)} %fusion), channel_id=2, replica_groups=mesh['dom'=32,'blk'=8] {'blk'}, use_global_device_ids=true, to_apply=%region_1.2.clone | all-reduce | flops 64 | bytes 512
  136.2 0.6 dynamic-slice.1
  136.8 0.0 copy-done
  (11 shorter events, 0.1 us)
Async XLA Ops:
  31.0 8.9 %copy-start.4 = (s32[16,6]{0,1:T(8,128)S(1)}, s32[16,6]{0,1:T(8,128)}, u32[]{:S(2)}) copy-start(s32[16,6]{0,1:T(8,128)} %param.16) | copy-start | bytes 1156
  31.1 9.7 %copy-start.1 = (bf16[192,3072]{1,0:T(8,128)(2,1)S(1)}, bf16[192,3072]{1,0:T(8,128)(2,1)}, u32[]{:S(2)}) copy-start(bf16[192,3072]{1,0:T(8,128)(2,1)} %param.15) | copy-start | bytes 3538948
  32.2 23.8 %all-to-all-start = ((bf16[32,64,192]{2,1,0:T(8,128)(2,1)}), bf16[32,64,192]{2,1,0:T(8,128)(2,1)}, u32[]{:S(2)}, u32[]{:S(2)}) async-start(bf16[32,64,192]{2,1,0:T(8,128)(2,1)} %broadcast_multiply_fusion.1), calls=%async_computation | async-start | bytes 2097152 | tf_op jit(solution)/shard_map/all_to_all | solution.py:13
  57.8 5.2 %copy-start.3 = (bf16[16,192]{1,0:T(8,128)(2,1)S(1)}, bf16[16,192]{1,0:T(8,128)(2,1)}, u32[]{:S(2)}) copy-start(bf16[16,192]{1,0:T(8,128)(2,1)} %param.12) | copy-start | bytes 18436
  89.2 6.2 %copy-start.2 = (bf16[128,192]{0,1:T(8,128)(2,1)S(1)}, bf16[128,192]{0,1:T(8,128)(2,1)}, u32[]{:S(2)}) copy-start(bf16[128,192]{0,1:T(8,128)(2,1)} %param.21) | copy-start | bytes 147460
  89.2 6.3 %copy-start.7 = (u32[256]{0:T(256)S(1)}, u32[256]{0:T(256)}, u32[]{:S(2)}) copy-start(u32[256]{0:T(256)} %constant.35) | copy-start | bytes 3076
  89.2 7.6 %copy-start.5 = (s32[128]{0:T(128)S(1)}, s32[128]{0:T(128)}, u32[]{:S(2)}) copy-start(s32[128]{0:T(128)} %param.19) | copy-start | bytes 1540
  90.3 21.3 %all-to-all-start.1 = ((bf16[32,64,192]{2,1,0:T(8,128)(2,1)}), bf16[32,64,192]{2,1,0:T(8,128)(2,1)S(1)}, u32[]{:S(2)}, u32[]{:S(2)}) async-start(bf16[32,64,192]{2,1,0:T(8,128)(2,1)} %broadcast_multiply_fusion), calls=%async_computation.1 | async-start | bytes 2097152 | tf_op jit(solution)/shard_map/all_to_all | solution.py:13
  117.7 1.9 %copy-start.6 = (s32[128]{0:T(128)S(1)}, s32[128]{0:T(128)}, u32[]{:S(2)}) copy-start(s32[128]{0:T(128)} %param.20) | copy-start | bytes 1540
  118.7 18.1 %copy-start = (f32[16,1,192]{2,0,1:T(8,128)}, f32[16,1,192]{2,0,1:T(8,128)S(1)}, u32[]{:S(2)}) copy-start(f32[16,1,192]{2,0,1:T(8,128)S(1)} %copy.43) | copy-start | bytes 36868
where the time goes:
time: 137 us
  blocking collectives  69.3 us (51%)
  waiting for transfers between devices  28.1 us (21%)
  starting transfers between devices  12.7 us (9%)
  matrix products  11.1 us (8%)
  local copies, waits for them, and re-layouts  8.15 us (6%)
  other arithmetic  4.47 us (3%)
  between operations  2.83 us (2%)
    all_gather x2, blocking collectives, extended_state(): partition = lax.all_gather(state, 'blk', axis=0, tiled=True)  52.9 us
    all_to_all x2, waiting for transfers between devices, cross_partition(): lax.all_to_all(outgoing, 'dom', split_axis=0, concat_axis=0, tiled=True)  28.1 us
    unnamed x1, blocking collectives  16.4 us
    all_to_all x2, starting transfers between devices, cross_partition(): lax.all_to_all(outgoing, 'dom', split_axis=0, concat_axis=0, tiled=True)  12.7 us
    dot_general x2, matrix products, sweep_once(): jnp.einsum('bim,bm->bi', offd, picked, preferred_element_type=jnp.float32)  10.3 us
  transfers between devices with their start and end apart: 2, of which 2 were waited for; matrix products, arithmetic and copies ran while one was open for 2% of the time, Pallas kernels for 0%

commit v1 on v0

--- a/solution.py
+++ b/solution.py
@@ -4,6 +4,38 @@
 from jax.sharding import PartitionSpec as P
 
 WP = 64
+
+
+def perform_sides(here_x, mesh_name, dimension_no):
+    opened, g_now, item_now = (
+        jax.lax.axis_size(mesh_name),
+        jax.lax.axis_index(mesh_name),
+        here_x.shape[dimension_no],
+    )
+    so_far_all = []
+    for rr, m in enumerate(here_x.shape):
+        so_far_all.append(m * opened if rr == dimension_no else m)
+    local_next = lax.dynamic_update_slice_in_dim(
+        jnp.zeros(so_far_all, here_x.dtype), here_x, g_now * item_now, axis=dimension_no
+    )
+    all_values = u1 = here_x
+    for to_i in [*range(1, opened // 2 + 1)]:
+        buffers = []
+        for rr in [*range(opened)]:
+            buffers.append((rr, (rr + 1) % opened))
+        all_values = jax.lax.ppermute(all_values, mesh_name, buffers)
+        local_next = lax.dynamic_update_slice_in_dim(
+            local_next, all_values, (g_now - to_i) % opened * item_now, axis=dimension_no
+        )
+        if 2 * to_i < opened:
+            grid = []
+            for rr in [*range(opened)]:
+                grid.append((rr, (rr - 1) % opened))
+            u1 = jax.lax.ppermute(u1, mesh_name, perm=grid)
+            local_next = lax.dynamic_update_slice_in_dim(
+                local_next, u1, (g_now + to_i) % opened * item_now, axis=dimension_no
+            )
+    return local_next
 
 
 def cross_partition(face_rows, partner_id):
@@ -16,7 +48,7 @@
 
 
 def extended_state(state, face_index, partner_id):
-    partition = lax.all_gather(state, "blk", axis=0, tiled=True)
+    partition = perform_sides(state, "blk", 0)
     halo_blocks = cross_partition(partition[face_index], partner_id)
     return jnp.concatenate([partition, halo_blocks], axis=0)
 

time: 137 us -> 124 us (0.905)
  blocking collectives: 69.3 us -> 14.2 us
  starting transfers between devices: 12.7 us -> 35.1 us
  waiting for transfers between devices: 28.1 us -> 45.9 us
    all_gather x2 -> x0, blocking collectives: 52.9 us -> none  [extended_state(): partition = lax.all_gather(state, 'blk', axis=0, tiled=True)]
    ppermute x0 -> x14, starting transfers between devices: none -> 22.3 us  [the longest x6 20.2 us: perform_sides(): u1 = jax.lax.ppermute(u1, mesh_name, perm=grid)]
    ppermute x0 -> x14, waiting for transfers between devices: none -> 17.8 us  [the longest x8 17.8 us: perform_sides(): all_values = jax.lax.ppermute(all_values, mesh_name, buffers)]
    unnamed x1, blocking collectives: 16.4 us -> 14.2 us
  transfers between devices with their start and end apart: 2 -> 16, of which waited for: 2 -> 9; matrix products, arithmetic and copies ran while one was open for 2% -> 3% of each run, Pallas kernels for 0% -> 0%
where the time goes in v1:
time: 124 us; the launch traced here: 123 us
  waiting for transfers between devices  45.9 us (37%)
  starting transfers between devices  35.1 us (28%)
  blocking collectives  14.2 us (11%)
  matrix products  11.1 us (9%)
  local copies, waits for them, and re-layouts  8.91 us (7%)
  other arithmetic  4.42 us (4%)
  between operations  2.92 us (2%)
    all_to_all x2, waiting for transfers between devices, cross_partition(): lax.all_to_all(outgoing, 'dom', split_axis=0, concat_axis=0, tiled=True)  28.1 us
    ppermute x6, starting transfers between devices, perform_sides(): u1 = jax.lax.ppermute(u1, mesh_name, perm=grid)  20.2 us
    ppermute x8, waiting for transfers between devices, perform_sides(): all_values = jax.lax.ppermute(all_values, mesh_name, buffers)  17.8 us
    unnamed x1, blocking collectives  14.2 us
    all_to_all x2, starting transfers between devices, cross_partition(): lax.all_to_all(outgoing, 'dom', split_axis=0, concat_axis=0, tiled=True)  12.7 us
    dot_general x2, matrix products, sweep_once(): jnp.einsum('bim,bm->bi', offd, picked, preferred_element_type=jnp.float32)  10.3 us
  transfers between devices with their start and end apart: 16, of which 9 were waited for; matrix products, arithmetic and copies ran while one was open for 3% of the time, Pallas kernels for 0%

profile of v1, /device:TPU:2, one launch (start us, length us, event | category | flops | bytes accessed | tf_op | source)
XLA Modules:
  0.0 122.5 jit_solution(13760470923677630754)
XLA Ops:
  0.6 2.0 %collective-permute-start = (bf16[16,192]{1,0:T(8,128)(2,1)}, bf16[16,192]{1,0:T(8,128)(2,1)S(1)}, u32[]{:S(2)}, u32[]{:S(2)}) collective-permute-start(bf16[16,192]{1,0:T(8,128)(2,1)} %param.13), channel_id=1, source_target_pairs={{0,1},{1,2},{2,3},{3,4},{4,5},{5,6},{6,7},{7,0},{8,9},{9,10},{10,1... | collective-permute-start | bytes 18440 | tf_op jit(solution)/shard_map/ppermute | solution.py:26
  2.6 4.0 %collective-permute-start.1 = (bf16[16,192]{1,0:T(8,128)(2,1)}, bf16[16,192]{1,0:T(8,128)(2,1)S(1)}, u32[]{:S(2)}, u32[]{:S(2)}) collective-permute-start(bf16[16,192]{1,0:T(8,128)(2,1)} %param.13), channel_id=1, source_target_pairs={{0,7},{1,0},{2,1},{3,2},{4,3},{5,4},{6,5},{7,6},{8,15},{9,8},{10,9... | collective-permute-start | bytes 18440 | tf_op jit(solution)/shard_map/ppermute | solution.py:34
  6.7 0.7 fusion.10
  8.0 0.7 constant_dynamic-update-slice_fusion.15
  8.7 0.0 collective-permute-done
  8.7 0.1 collective-permute-start.2
  8.8 0.0 collective-permute-done.1
  8.8 3.2 %collective-permute-start.3 = (bf16[16,192]{1,0:T(8,128)(2,1)S(1)}, bf16[16,192]{1,0:T(8,128)(2,1)S(1)}, u32[]{:S(2)}, u32[]{:S(2)}) collective-permute-start(bf16[16,192]{1,0:T(8,128)(2,1)S(1)} %collective-permute-done.1), channel_id=1, source_target_pairs={{0,7},{1,0},{2,1},{3,2},{4,3},{5,4},{6,5},{7,6},{8,15},{9,8},{10,9... | collective-permute-start | bytes 18440 | tf_op jit(solution)/shard_map/ppermute | solution.py:34
  12.0 1.6 %collective-permute-done.2 = bf16[16,192]{1,0:T(8,128)(2,1)S(1)} collective-permute-done((bf16[16,192]{1,0:T(8,128)(2,1)S(1)}, bf16[16,192]{1,0:T(8,128)(2,1)S(1)}, u32[]{:S(2)}, u32[]{:S(2)}) %collective-permute-start.2) | collective-permute-done | bytes 6176 | tf_op jit(solution)/shard_map/ppermute | solution.py:26
  13.6 0.0 collective-permute-start.4
  13.6 0.0 collective-permute-done.3
  13.6 3.2 %collective-permute-start.5 = (bf16[16,192]{1,0:T(8,128)(2,1)S(1)}, bf16[16,192]{1,0:T(8,128)(2,1)S(1)}, u32[]{:S(2)}, u32[]{:S(2)}) collective-permute-start(bf16[16,192]{1,0:T(8,128)(2,1)S(1)} %collective-permute-done.3), channel_id=1, source_target_pairs={{0,7},{1,0},{2,1},{3,2},{4,3},{5,4},{6,5},{7,6},{8,15},{9,8},{10,9... | collective-permute-start | bytes 18440 | tf_op jit(solution)/shard_map/ppermute | solution.py:34
  16.9 1.6 %collective-permute-done.4 = bf16[16,192]{1,0:T(8,128)(2,1)S(1)} collective-permute-done((bf16[16,192]{1,0:T(8,128)(2,1)S(1)}, bf16[16,192]{1,0:T(8,128)(2,1)S(1)}, u32[]{:S(2)}, u32[]{:S(2)}) %collective-permute-start.4) | collective-permute-done | bytes 6176 | tf_op jit(solution)/shard_map/ppermute | solution.py:26
  18.5 0.0 collective-permute-start.6
  18.5 4.8 %collective-permute-done.6 = bf16[16,192]{1,0:T(8,128)(2,1)S(1)} collective-permute-done((bf16[16,192]{1,0:T(8,128)(2,1)S(1)}, bf16[16,192]{1,0:T(8,128)(2,1)S(1)}, u32[]{:S(2)}, u32[]{:S(2)}) %collective-permute-start.6) | collective-permute-done | bytes 6176 | tf_op jit(solution)/shard_map/ppermute | solution.py:26
  23.4 0.7 gather_fusion
  24.1 0.0 copy-start.4
  24.1 0.0 copy-start.1
  24.1 1.1 broadcast_multiply_fusion.1
  25.2 7.7 %all-to-all-start = ((bf16[32,64,192]{2,1,0:T(8,128)(2,1)}), bf16[32,64,192]{2,1,0:T(8,128)(2,1)}, u32[]{:S(2)}, u32[]{:S(2)}) async-start(bf16[32,64,192]{2,1,0:T(8,128)(2,1)} %broadcast_multiply_fusion.1), calls=%async_computation | async-start | bytes 2097152 | tf_op jit(solution)/shard_map/all_to_all | solution.py:45
  32.9 0.1 copy.18
  33.0 0.1 reshape.62
  33.8 0.7 copy.29
  34.4 1.3 %dynamic_slice.11 = f32[1]{0:T(128)} dynamic-slice(f32[1024]{0:T(1024)} %param.22, s32[]{:T(128)S(6)} %select_n.104), dynamic_slice_sizes={1} | dynamic-slice | bytes 12 | tf_op jit(solution)/shard_map/jit(dynamic_index_in_dim)/dynamic_slice | solution.py:78
  35.7 13.3 %all-to-all-done = bf16[32,64,192]{2,1,0:T(8,128)(2,1)} async-done(((bf16[32,64,192]{2,1,0:T(8,128)(2,1)}), bf16[32,64,192]{2,1,0:T(8,128)(2,1)}, u32[]{:S(2)}, u32[]{:S(2)}) %all-to-all-start) | async-done | bytes 786464 | tf_op jit(solution)/shard_map/all_to_all | solution.py:45
  49.0 0.8 dynamic-slice_bitcast_fusion.1
  49.8 0.8 gather_fusion.1
  50.6 0.1 reshape.110
  50.7 0.0 copy-start.3
  50.7 5.2 %fusion.12 = f32[16,1,192]{2,1,0:T(1,128)S(1)} fusion(bf16[16,1152,1]{1,2,0:T(2,128)(2,1)S(1)} %reshape.110, bf16[16,192,1152]{2,1,0:T(8,128)(2,1)} %param.14), kind=kOutput, calls=%fused_computation.54 | convolution fusion | flops 7077888 | bytes 7127040 | tf_op jit(solution)/shard_map/bim,bm->bi/dot_general | solution.py:59
  55.9 0.7 fusion.8
  56.6 0.3 fusion.6
  56.9 0.1 collective-permute-start.7
  57.0 3.2 %collective-permute-start.8 = (bf16[16,192]{1,0:T(8,128)(2,1)S(1)}, bf16[16,192]{1,0:T(8,128)(2,1)S(1)}, u32[]{:S(2)}, u32[]{:S(2)}) collective-permute-start(bf16[16,192]{1,0:T(8,128)(2,1)S(1)} %get-tuple-element.3), channel_id=1, source_target_pairs={{0,7},{1,0},{2,1},{3,2},{4,3},{5,4},{6,5},{7,6},{8,15},{9,8},{10,9... | collective-permute-start | bytes 18440 | tf_op jit(solution)/shard_map/ppermute | solution.py:34
  60.2 1.6 %collective-permute-done.7 = bf16[16,192]{1,0:T(8,128)(2,1)S(1)} collective-permute-done((bf16[16,192]{1,0:T(8,128)(2,1)S(1)}, bf16[16,192]{1,0:T(8,128)(2,1)S(1)}, u32[]{:S(2)}, u32[]{:S(2)}) %collective-permute-start.7) | collective-permute-done | bytes 6176 | tf_op jit(solution)/shard_map/ppermute | solution.py:26
  61.9 0.0 collective-permute-start.9
  61.9 3.2 %collective-permute-start.10 = (bf16[16,192]{1,0:T(8,128)(2,1)S(1)}, bf16[16,192]{1,0:T(8,128)(2,1)S(1)}, u32[]{:S(2)}, u32[]{:S(2)}) collective-permute-start(bf16[16,192]{1,0:T(8,128)(2,1)S(1)} %collective-permute-done.8), channel_id=1, source_target_pairs={{0,7},{1,0},{2,1},{3,2},{4,3},{5,4},{6,5},{7,6},{8,15},{9,8},{10,9... | collective-permute-start | bytes 18440 | tf_op jit(solution)/shard_map/ppermute | solution.py:34
  65.1 1.6 %collective-permute-done.9 = bf16[16,192]{1,0:T(8,128)(2,1)S(1)} collective-permute-done((bf16[16,192]{1,0:T(8,128)(2,1)S(1)}, bf16[16,192]{1,0:T(8,128)(2,1)S(1)}, u32[]{:S(2)}, u32[]{:S(2)}) %collective-permute-start.9) | collective-permute-done | bytes 6176 | tf_op jit(solution)/shard_map/ppermute | solution.py:26
  66.7 0.0 collective-permute-start.11
  66.7 0.0 collective-permute-done.10
  66.7 3.2 %collective-permute-start.12 = (bf16[16,192]{1,0:T(8,128)(2,1)S(1)}, bf16[16,192]{1,0:T(8,128)(2,1)S(1)}, u32[]{:S(2)}, u32[]{:S(2)}) collective-permute-start(bf16[16,192]{1,0:T(8,128)(2,1)S(1)} %collective-permute-done.10), channel_id=1, source_target_pairs={{0,7},{1,0},{2,1},{3,2},{4,3},{5,4},{6,5},{7,6},{8,15},{9,8},{10,9... | collective-permute-start | bytes 18440 | tf_op jit(solution)/shard_map/ppermute | solution.py:34
  70.0 1.6 %collective-permute-done.11 = bf16[16,192]{1,0:T(8,128)(2,1)S(1)} collective-permute-done((bf16[16,192]{1,0:T(8,128)(2,1)S(1)}, bf16[16,192]{1,0:T(8,128)(2,1)S(1)}, u32[]{:S(2)}, u32[]{:S(2)}) %collective-permute-start.11) | collective-permute-done | bytes 6176 | tf_op jit(solution)/shard_map/ppermute | solution.py:26
  71.6 0.0 collective-permute-start.13
  71.6 0.0 collective-permute-done.12
  71.6 4.8 %collective-permute-done.13 = bf16[16,192]{1,0:T(8,128)(2,1)S(1)} collective-permute-done((bf16[16,192]{1,0:T(8,128)(2,1)S(1)}, bf16[16,192]{1,0:T(8,128)(2,1)S(1)}, u32[]{:S(2)}, u32[]{:S(2)}) %collective-permute-start.13) | collective-permute-done | bytes 6176 | tf_op jit(solution)/shard_map/ppermute | solution.py:26
  76.4 0.7 gather_fusion.2
  77.1 0.0 copy-start.2
  77.2 0.0 copy-start.7
  77.2 0.0 copy-start.5
  77.2 1.1 broadcast_multiply_fusion
  78.3 5.0 %all-to-all-start.1 = ((bf16[32,64,192]{2,1,0:T(8,128)(2,1)}), bf16[32,64,192]{2,1,0:T(8,128)(2,1)S(1)}, u32[]{:S(2)}, u32[]{:S(2)}) async-start(bf16[32,64,192]{2,1,0:T(8,128)(2,1)} %broadcast_multiply_fusion), calls=%async_computation.1 | async-start | bytes 2097152 | tf_op jit(solution)/shard_map/all_to_all | solution.py:45
  83.4 0.1 copy.19
  83.5 0.6 dynamic-slice
  84.8 14.8 %all-to-all-done.1 = bf16[32,64,192]{2,1,0:T(8,128)(2,1)S(1)} async-done(((bf16[32,64,192]{2,1,0:T(8,128)(2,1)}), bf16[32,64,192]{2,1,0:T(8,128)(2,1)S(1)}, u32[]{:S(2)}, u32[]{:S(2)}) %all-to-all-start.1) | async-done | bytes 786464 | tf_op jit(solution)/shard_map/all_to_all | solution.py:45
  99.6 0.8 gather_fusion.3
  100.4 0.1 reshape.112
  100.5 5.2 %fusion.13 = f32[16,1,192]{2,1,0:T(1,128)S(1)} fusion(bf16[16,1152,1]{1,2,0:T(2,128)(2,1)S(1)} %reshape.112, bf16[16,192,1152]{2,1,0:T(8,128)(2,1)} %param.14), kind=kOutput, calls=%fused_computation.55 | convolution fusion | flops 7077888 | bytes 7127040 | tf_op jit(solution)/shard_map/bim,bm->bi/dot_general | solution.py:59
  105.7 0.7 fusion.9
  106.3 0.3 fusion.4
  106.7 0.8 gather_fusion.4
  107.4 0.1 multiply_reduce_fusion
  107.6 0.2 fusion
  107.7 14.2 %all-reduce = f32[64]{0:T(128)S(1)} all-reduce(f32[64]{0:T(128)S(1)} %fusion), channel_id=2, replica_groups=mesh['dom'=32,'blk'=8] {'blk'}, use_global_device_ids=true, to_apply=%region_1.2.clone | all-reduce | flops 64 | bytes 512
  121.9 0.6 dynamic-slice.1
  (39 shorter events, 0.2 us)
Async XLA Ops:
  0.6 8.1 %collective-permute-start = (bf16[16,192]{1,0:T(8,128)(2,1)}, bf16[16,192]{1,0:T(8,128)(2,1)S(1)}, u32[]{:S(2)}, u32[]{:S(2)}) collective-permute-start(bf16[16,192]{1,0:T(8,128)(2,1)} %param.13), channel_id=1, source_target_pairs={{0,1},{1,2},{2,3},{3,4},{4,5},{5,6},{6,7},{7,0},{8,9},{9,10},{10,1... | collective-permute-start | bytes 18440 | tf_op jit(solution)/shard_map/ppermute | solution.py:26
  2.6 6.2 %collective-permute-start.1 = (bf16[16,192]{1,0:T(8,128)(2,1)}, bf16[16,192]{1,0:T(8,128)(2,1)S(1)}, u32[]{:S(2)}, u32[]{:S(2)}) collective-permute-start(bf16[16,192]{1,0:T(8,128)(2,1)} %param.13), channel_id=1, source_target_pairs={{0,7},{1,0},{2,1},{3,2},{4,3},{5,4},{6,5},{7,6},{8,15},{9,8},{10,9... | collective-permute-start | bytes 18440 | tf_op jit(solution)/shard_map/ppermute | solution.py:34
  8.7 4.9 %collective-permute-start.2 = (bf16[16,192]{1,0:T(8,128)(2,1)S(1)}, bf16[16,192]{1,0:T(8,128)(2,1)S(1)}, u32[]{:S(2)}, u32[]{:S(2)}) collective-permute-start(bf16[16,192]{1,0:T(8,128)(2,1)S(1)} %collective-permute-done), channel_id=1, source_target_pairs={{0,1},{1,2},{2,3},{3,4},{4,5},{5,6},{6,7},{7,0},{8,9},{9,10},{10,1... | collective-permute-start | bytes 18440 | tf_op jit(solution)/shard_map/ppermute | solution.py:26
  8.8 4.8 %collective-permute-start.3 = (bf16[16,192]{1,0:T(8,128)(2,1)S(1)}, bf16[16,192]{1,0:T(8,128)(2,1)S(1)}, u32[]{:S(2)}, u32[]{:S(2)}) collective-permute-start(bf16[16,192]{1,0:T(8,128)(2,1)S(1)} %collective-permute-done.1), channel_id=1, source_target_pairs={{0,7},{1,0},{2,1},{3,2},{4,3},{5,4},{6,5},{7,6},{8,15},{9,8},{10,9... | collective-permute-start | bytes 18440 | tf_op jit(solution)/shard_map/ppermute | solution.py:34
  13.6 4.9 %collective-permute-start.4 = (bf16[16,192]{1,0:T(8,128)(2,1)S(1)}, bf16[16,192]{1,0:T(8,128)(2,1)S(1)}, u32[]{:S(2)}, u32[]{:S(2)}) collective-permute-start(bf16[16,192]{1,0:T(8,128)(2,1)S(1)} %collective-permute-done.2), channel_id=1, source_target_pairs={{0,1},{1,2},{2,3},{3,4},{4,5},{5,6},{6,7},{7,0},{8,9},{9,10},{10,1... | collective-permute-start | bytes 18440 | tf_op jit(solution)/shard_map/ppermute | solution.py:26
  13.6 4.9 %collective-permute-start.5 = (bf16[16,192]{1,0:T(8,128)(2,1)S(1)}, bf16[16,192]{1,0:T(8,128)(2,1)S(1)}, u32[]{:S(2)}, u32[]{:S(2)}) collective-permute-start(bf16[16,192]{1,0:T(8,128)(2,1)S(1)} %collective-permute-done.3), channel_id=1, source_target_pairs={{0,7},{1,0},{2,1},{3,2},{4,3},{5,4},{6,5},{7,6},{8,15},{9,8},{10,9... | collective-permute-start | bytes 18440 | tf_op jit(solution)/shard_map/ppermute | solution.py:34
  18.5 4.9 %collective-permute-start.6 = (bf16[16,192]{1,0:T(8,128)(2,1)S(1)}, bf16[16,192]{1,0:T(8,128)(2,1)S(1)}, u32[]{:S(2)}, u32[]{:S(2)}) collective-permute-start(bf16[16,192]{1,0:T(8,128)(2,1)S(1)} %collective-permute-done.4), channel_id=1, source_target_pairs={{0,1},{1,2},{2,3},{3,4},{4,5},{5,6},{6,7},{7,0},{8,9},{9,10},{10,1... | collective-permute-start | bytes 18440 | tf_op jit(solution)/shard_map/ppermute | solution.py:26
  24.1 8.8 %copy-start.4 = (s32[16,6]{0,1:T(8,128)S(1)}, s32[16,6]{0,1:T(8,128)}, u32[]{:S(2)}) copy-start(s32[16,6]{0,1:T(8,128)} %param.16) | copy-start | bytes 1156
  24.1 9.7 %copy-start.1 = (bf16[192,3072]{1,0:T(8,128)(2,1)S(1)}, bf16[192,3072]{1,0:T(8,128)(2,1)}, u32[]{:S(2)}) copy-start(bf16[192,3072]{1,0:T(8,128)(2,1)} %param.15) | copy-start | bytes 3538948
  25.2 23.8 %all-to-all-start = ((bf16[32,64,192]{2,1,0:T(8,128)(2,1)}), bf16[32,64,192]{2,1,0:T(8,128)(2,1)}, u32[]{:S(2)}, u32[]{:S(2)}) async-start(bf16[32,64,192]{2,1,0:T(8,128)(2,1)} %broadcast_multiply_fusion.1), calls=%async_computation | async-start | bytes 2097152 | tf_op jit(solution)/shard_map/all_to_all | solution.py:45
  50.7 5.2 %copy-start.3 = (bf16[16,192]{1,0:T(8,128)(2,1)S(1)}, bf16[16,192]{1,0:T(8,128)(2,1)}, u32[]{:S(2)}) copy-start(bf16[16,192]{1,0:T(8,128)(2,1)} %param.12) | copy-start | bytes 18436
  56.9 4.9 %collective-permute-start.7 = (bf16[16,192]{1,0:T(8,128)(2,1)S(1)}, bf16[16,192]{1,0:T(8,128)(2,1)S(1)}, u32[]{:S(2)}, u32[]{:S(2)}) collective-permute-start(bf16[16,192]{1,0:T(8,128)(2,1)S(1)} %get-tuple-element.3), channel_id=1, source_target_pairs={{0,1},{1,2},{2,3},{3,4},{4,5},{5,6},{6,7},{7,0},{8,9},{9,10},{10,1... | collective-permute-start | bytes 18440 | tf_op jit(solution)/shard_map/ppermute | solution.py:26
  57.0 4.9 %collective-permute-start.8 = (bf16[16,192]{1,0:T(8,128)(2,1)S(1)}, bf16[16,192]{1,0:T(8,128)(2,1)S(1)}, u32[]{:S(2)}, u32[]{:S(2)}) collective-permute-start(bf16[16,192]{1,0:T(8,128)(2,1)S(1)} %get-tuple-element.3), channel_id=1, source_target_pairs={{0,7},{1,0},{2,1},{3,2},{4,3},{5,4},{6,5},{7,6},{8,15},{9,8},{10,9... | collective-permute-start | bytes 18440 | tf_op jit(solution)/shard_map/ppermute | solution.py:34
  61.9 4.9 %collective-permute-start.9 = (bf16[16,192]{1,0:T(8,128)(2,1)S(1)}, bf16[16,192]{1,0:T(8,128)(2,1)S(1)}, u32[]{:S(2)}, u32[]{:S(2)}) collective-permute-start(bf16[16,192]{1,0:T(8,128)(2,1)S(1)} %collective-permute-done.7), channel_id=1, source_target_pairs={{0,1},{1,2},{2,3},{3,4},{4,5},{5,6},{6,7},{7,0},{8,9},{9,10},{10,1... | collective-permute-start | bytes 18440 | tf_op jit(solution)/shard_map/ppermute | solution.py:26
  61.9 4.9 %collective-permute-start.10 = (bf16[16,192]{1,0:T(8,128)(2,1)S(1)}, bf16[16,192]{1,0:T(8,128)(2,1)S(1)}, u32[]{:S(2)}, u32[]{:S(2)}) collective-permute-start(bf16[16,192]{1,0:T(8,128)(2,1)S(1)} %collective-permute-done.8), channel_id=1, source_target_pairs={{0,7},{1,0},{2,1},{3,2},{4,3},{5,4},{6,5},{7,6},{8,15},{9,8},{10,9... | collective-permute-start | bytes 18440 | tf_op jit(solution)/shard_map/ppermute | solution.py:34
  66.7 4.9 %collective-permute-start.11 = (bf16[16,192]{1,0:T(8,128)(2,1)S(1)}, bf16[16,192]{1,0:T(8,128)(2,1)S(1)}, u32[]{:S(2)}, u32[]{:S(2)}) collective-permute-start(bf16[16,192]{1,0:T(8,128)(2,1)S(1)} %collective-permute-done.9), channel_id=1, source_target_pairs={{0,1},{1,2},{2,3},{3,4},{4,5},{5,6},{6,7},{7,0},{8,9},{9,10},{10,1... | collective-permute-start | bytes 18440 | tf_op jit(solution)/shard_map/ppermute | solution.py:26
  66.7 4.9 %collective-permute-start.12 = (bf16[16,192]{1,0:T(8,128)(2,1)S(1)}, bf16[16,192]{1,0:T(8,128)(2,1)S(1)}, u32[]{:S(2)}, u32[]{:S(2)}) collective-permute-start(bf16[16,192]{1,0:T(8,128)(2,1)S(1)} %collective-permute-done.10), channel_id=1, source_target_pairs={{0,7},{1,0},{2,1},{3,2},{4,3},{5,4},{6,5},{7,6},{8,15},{9,8},{10,9... | collective-permute-start | bytes 18440 | tf_op jit(solution)/shard_map/ppermute | solution.py:34
  71.6 4.9 %collective-permute-start.13 = (bf16[16,192]{1,0:T(8,128)(2,1)S(1)}, bf16[16,192]{1,0:T(8,128)(2,1)S(1)}, u32[]{:S(2)}, u32[]{:S(2)}) collective-permute-start(bf16[16,192]{1,0:T(8,128)(2,1)S(1)} %collective-permute-done.11), channel_id=1, source_target_pairs={{0,1},{1,2},{2,3},{3,4},{4,5},{5,6},{6,7},{7,0},{8,9},{9,10},{10,1... | collective-permute-start | bytes 18440 | tf_op jit(solution)/shard_map/ppermute | solution.py:26
  77.1 6.2 %copy-start.2 = (bf16[128,192]{0,1:T(8,128)(2,1)S(1)}, bf16[128,192]{0,1:T(8,128)(2,1)}, u32[]{:S(2)}) copy-start(bf16[128,192]{0,1:T(8,128)(2,1)} %param.21) | copy-start | bytes 147460
  77.2 6.3 %copy-start.7 = (u32[256]{0:T(256)S(1)}, u32[256]{0:T(256)}, u32[]{:S(2)}) copy-start(u32[256]{0:T(256)} %constant.109) | copy-start | bytes 3076
  77.2 7.6 %copy-start.5 = (s32[128]{0:T(128)S(1)}, s32[128]{0:T(128)}, u32[]{:S(2)}) copy-start(s32[128]{0:T(128)} %param.19) | copy-start | bytes 1540
  78.3 21.3 %all-to-all-start.1 = ((bf16[32,64,192]{2,1,0:T(8,128)(2,1)}), bf16[32,64,192]{2,1,0:T(8,128)(2,1)S(1)}, u32[]{:S(2)}, u32[]{:S(2)}) async-start(bf16[32,64,192]{2,1,0:T(8,128)(2,1)} %broadcast_multiply_fusion), calls=%async_computation.1 | async-start | bytes 2097152 | tf_op jit(solution)/shard_map/all_to_all | solution.py:45
  105.7 1.9 %copy-start.6 = (s32[128]{0:T(128)S(1)}, s32[128]{0:T(128)}, u32[]{:S(2)}) copy-start(s32[128]{0:T(128)} %param.20) | copy-start | bytes 1540
  106.7 15.8 %copy-start = (f32[16,1,192]{2,0,1:T(8,128)}, f32[16,1,192]{2,0,1:T(8,128)S(1)}, u32[]{:S(2)}) copy-start(f32[16,1,192]{2,0,1:T(8,128)S(1)} %copy.43) | copy-start | bytes 36868
